TPU v7x, 512 devices: a whole 4x4x16 slice. The times are simulated.
512 devices in a mesh: tm: 8 (over z_hi, core), tile: 16 (over x, y), head: 4 (over z_lo).
Axes of the slice: x: 4, y: 4, z: 16 (z_hi: 4, z_lo: 4; z = z_hi * 4 + z_lo), core: 2. Of those that a mesh axis runs over, the one named last changes fastest.
Arguments:
- query: bfloat16 [8, 16, 2, 16, 16, 1536], P('tm', 'tile', None, None, None, 'head'), may hold values from -80 to 80
- keys: bfloat16 [8, 16, 2, 16, 16, 1536], P('tm', 'tile', None, None, None, 'head'), may hold values from -80 to 80
- values: bfloat16 [8, 16, 2, 16, 16, 1536], P('tm', 'tile', None, None, None, 'head'), may hold values from -6 to 6
- out_weight: bfloat16 [1536, 1536], P('head'), may hold values from -0.15625 to 0.15625
- radius: int32 [12], P('head'), may hold values from 1 to 4
- block_mask: int32 [12, 8, 8], P('head'), may hold values from 0 to 1, as said below
Outputs:
- mixed: bfloat16 [8, 16, 512, 1536], P('tm', 'tile', 'head')
Inputs may be any that keep to these rules, and one draw needn't show every extreme that they name: For every head, block_mask is 1 on the diagonal of its table and 0 above it.
All inputs are finite; a program needn't handle non-finite values.
Results may differ from a plain program's by a relative error of at most 0.015.
Values may be sent and summed in bfloat16 or wider, within the bound.
A program may use at most 128 MiB of HBM per device.

v0:
```python
import math
import jax
import jax.numpy as jnp
from jax import lax
from jax.sharding import PartitionSpec as P

RMAX = 4


def passed_along(value, axis, by):
    peers = lax.axis_size(axis)
    pairs = [(i, i + by) for i in range(peers) if 0 <= i + by < peers]
    return lax.ppermute(value, axis, pairs)


def widen(key_part, value_part, span, row_move, col_move):
    grid = math.isqrt(lax.axis_size("tile"))
    above = None
    below = None
    for offset in (grid, -grid):
        if offset > 0:
            face_key = key_part[:, :, key_part.shape[2] - span :]
            face_value = value_part[:, :, value_part.shape[2] - span :]
        else:
            face_key = key_part[:, :, :span]
            face_value = value_part[:, :, :span]
        got = row_move(face_key, face_value, offset)
        if offset > 0:
            above = got
        else:
            below = got
    key_rows = jnp.concatenate([above[0], key_part, below[0]], axis=2)
    value_rows = jnp.concatenate([above[1], value_part, below[1]], axis=2)
    left = None
    right = None
    for offset in (1, -1):
        if offset > 0:
            face_key = key_rows[:, :, :, key_rows.shape[3] - span :]
            face_value = value_rows[:, :, :, value_rows.shape[3] - span :]
        else:
            face_key = key_rows[:, :, :, :span]
            face_value = value_rows[:, :, :, :span]
        got = col_move(face_key, face_value, offset)
        if offset > 0:
            left = got
        else:
            right = got
    key_full = jnp.concatenate([left[0], key_rows, right[0]], axis=3)
    value_full = jnp.concatenate([left[1], value_rows, right[1]], axis=3)
    return (key_full, value_full)


def windows_of(block, half_high, half_wide, win_high, win_wide, heads_here, head_dim):
    parts = []
    for band in (0, 1):
        for strip in (0, 1):
            parts.append(
                block[
                    :,
                    band * half_high : band * half_high + win_high,
                    strip * half_wide : strip * half_wide + win_wide,
                ]
            )
    stacked = jnp.stack(parts)
    return stacked.reshape(4, -1, heads_here, head_dim)


def per_device(query, keys, values, out_weight, radius, block_mask):
    span = RMAX
    grid = math.isqrt(lax.axis_size("tile"))
    tile_at = lax.axis_index("tile")
    row_at = tile_at // grid
    col_at = tile_at % grid
    stretch_at = lax.axis_index("tm")
    frames, high, wide, channels = query.shape[2:]
    heads_here = radius.shape[0]
    head_dim = channels // heads_here
    tokens_here = frames * high * wide
    half_high = high // 2
    half_wide = wide // 2
    win_high = half_high + 2 * span
    win_wide = half_wide + 2 * span
    quarter = frames * half_high * half_wide
    queries = query[0, 0].reshape(frames, 2, half_high, 2, half_wide, channels)
    queries = queries.transpose(1, 3, 0, 2, 4, 5).reshape(4, quarter, heads_here, head_dim)
    query_y = jnp.broadcast_to(
        jnp.arange(half_high, dtype=jnp.int32)[None, :, None], (frames, half_high, half_wide)
    ).reshape(-1)
    query_x = jnp.broadcast_to(
        jnp.arange(half_wide, dtype=jnp.int32)[None, None, :], (frames, half_high, half_wide)
    ).reshape(-1)
    key_y = jnp.broadcast_to(
        jnp.arange(win_high, dtype=jnp.int32)[None, :, None] - span, (frames, win_high, win_wide)
    ).reshape(-1)
    key_x = jnp.broadcast_to(
        jnp.arange(win_wide, dtype=jnp.int32)[None, None, :] - span, (frames, win_high, win_wide)
    ).reshape(-1)
    band_at = jnp.array([0, 0, 1, 1], dtype=jnp.int32)
    strip_at = jnp.array([0, 1, 0, 1], dtype=jnp.int32)
    global_y = row_at * high + band_at[:, None] * half_high + key_y[None, :]
    global_x = col_at * wide + strip_at[:, None] * half_wide + key_x[None, :]
    inside = (global_y >= 0) & (global_y < grid * high) & (global_x >= 0) & (global_x < grid * wide)
    distance = jnp.maximum(
        jnp.abs(query_y[:, None] - key_y[None, :]), jnp.abs(query_x[:, None] - key_x[None, :])
    )
    near = distance[None, :, :] <= radius[:, None, None]
    allowed = near[None, :, :, :] & inside[:, None, None, :]
    scale = 1.0 / math.sqrt(head_dim)
    initial = (
        jnp.full((4, heads_here, quarter), -1e30, jnp.float32),
        jnp.zeros((4, heads_here, quarter), jnp.float32),
        jnp.zeros((4, heads_here, quarter, head_dim), jnp.float32),
    )

    def all_row_move(face_key, face_value, offset):
        return passed_along((face_key, face_value), "tile", offset)

    def all_col_move(face_key, face_value, offset):
        return passed_along((face_key, face_value), "tile", offset)

    key_all, value_all = (
        lax.all_gather(keys[0], "tm", axis=0, tiled=True),
        lax.all_gather(values[0], "tm", axis=0, tiled=True),
    )
    key_full, value_full = widen(key_all, value_all, span, all_row_move, all_col_move)
    piece = (key_full, value_full)
    count = piece[0].shape[0]
    stretch_ids = jnp.arange(count, dtype=jnp.int32)

    def one_stretch(state, item):
        key_block, value_block, stretch_id = item
        visible = (
            lax.dynamic_slice_in_dim(
                lax.dynamic_index_in_dim(block_mask, stretch_at, 1, False), stretch_id, 1, 1
            )[:, 0]
            > 0
        )
        best, total, acc = state
        key_win = windows_of(
            key_block, half_high, half_wide, win_high, win_wide, heads_here, head_dim
        )
        value_win = windows_of(
            value_block, half_high, half_wide, win_high, win_wide, heads_here, head_dim
        )
        usable = allowed & visible[None, :, None, None]
        scores = (
            jnp.einsum("nqhd,nkhd->nhqk", queries, key_win, preferred_element_type=jnp.float32)
            * scale
        )
        masked = jnp.where(usable, scores, jnp.float32(-1e30))
        fresh = jnp.maximum(best, jnp.max(masked, axis=3))
        probs = jnp.where(usable, jnp.exp(scores - fresh[..., None]), jnp.float32(0.0))
        shrink = jnp.exp(best - fresh)
        total = total * shrink + jnp.sum(probs, axis=3)
        acc = acc * shrink[..., None] + jnp.einsum(
            "nhqk,nkhd->nhqd",
            probs.astype(jnp.bfloat16),
            value_win,
            preferred_element_type=jnp.float32,
        )
        result = (fresh, total, acc)
        return (result, None)

    final, unused = lax.scan(one_stretch, initial, (piece[0], piece[1], stretch_ids))
    best, total, acc = final
    attn = (acc / total[..., None]).astype(jnp.bfloat16)
    attn = attn.transpose(0, 2, 1, 3).reshape(
        2, 2, frames, half_high, half_wide, heads_here * head_dim
    )
    attn = attn.transpose(2, 0, 3, 1, 4, 5).reshape(tokens_here, heads_here * head_dim)
    mixed = lax.psum_scatter(
        jnp.dot(attn, out_weight, preferred_element_type=jnp.float32).astype(jnp.bfloat16),
        "head",
        scatter_dimension=0,
        tiled=True,
    )
    return mixed.reshape(1, 1, -1, out_weight.shape[1])


def solution(mesh):
    in_specs = (
        P("tm", "tile", None, None, None, "head"),
        P("tm", "tile", None, None, None, "head"),
        P("tm", "tile", None, None, None, "head"),
        P("head", None),
        P("head"),
        P("head", None, None),
    )
    out_specs = P("tm", "tile", "head", None)
    return jax.shard_map(
        per_device, mesh=mesh, in_specs=in_specs, out_specs=out_specs, check_vma=False
    )
```

profile of v0, /device:TPU:1, one launch (start us, length us, event | category | flops | bytes accessed | tf_op | source)
XLA Modules:
  0.0 517.4 jit_solution(15858110646869679896)
XLA Ops:
  8.1 85.1 %all-gather.7.cloned.1.call-done = bf16[8,1,2,16,16,384]{5,4,3,2,1,0:T(8,128)(2,1)} async-done(((bf16[1,1,2,16,16,384]{5,4,3,2,1,0:T(8,128)(2,1)}), bf16[8,1,2,16,16,384]{5,4,3,2,1,0:T(8,128)(2,1)}) %all-gather.7.cloned.1.call-update) | async-done | bytes 3145744 | tf_op jit(solution)/shard_map/all_gather | solution.py:123
  102.1 14.4 %collective-permute-done.4 = bf16[8,2,4,16,384]{4,3,2,1,0:T(8,128)(2,1)S(1)} collective-permute-done((bf16[8,2,4,16,384]{4,3,2,1,0:T(8,128)(2,1)}, bf16[8,2,4,16,384]{4,3,2,1,0:T(8,128)(2,1)S(1)}, u32[]{:S(2)}, u32[]{:S(2)}) %collective-permute-start.4) | collective-permute-done | bytes 786464 | tf_op jit(solution)/shard_map/ppermute | solution.py:13
  123.6 4.2 collective-permute-start.6
  129.0 40.4 %all-gather.5.cloned.1.call-done = bf16[8,1,2,16,16,384]{5,4,3,2,1,0:T(8,128)(2,1)} async-done(((bf16[1,1,2,16,16,384]{5,4,3,2,1,0:T(8,128)(2,1)}), bf16[8,1,2,16,16,384]{5,4,3,2,1,0:T(8,128)(2,1)}) %all-gather.5.cloned.1.call-update) | async-done | bytes 3145744 | tf_op jit(solution)/shard_map/all_gather | solution.py:122
  205.1 7.7 %pad_maximum_fusion.1 = bf16[8,2,24,24,384]{4,3,2,1,0:T(8,128)(2,1)} fusion(bf16[8,2,24,4,384]{4,3,2,1,0:T(4,128)(2,1)} %collective-permute-done.7, bf16[8,2,4,16,384]{4,3,2,1,0:T(8,128)(2,1)S(1)} %collective-permute-done.5, bf16[8,2,16,16,384]{4,3,2,1,0:T(8,128)(2,1)S(1)} %bitcast.74, bf16[8,2,4,16,384]{4,3,2,1,0:T(8,128)(2,1)S(1)} %collective-permute-done.4, ...), kind=kLoop, calls=%fused_computation.46 | loop fusion | flops 35389440 | bytes 14155776 | tf_op jit(solution)/shard_map/concatenate | solution.py:49
  212.8 14.5 %collective-permute-done.2 = bf16[8,2,24,4,384]{4,3,2,1,0:T(4,128)(2,1)S(1)} collective-permute-done((bf16[8,2,24,4,384]{4,3,2,1,0:T(4,128)(2,1)S(1)}, bf16[8,2,24,4,384]{4,3,2,1,0:T(4,128)(2,1)S(1)}, u32[]{:S(2)}, u32[]{:S(2)}) %collective-permute-start.2) | collective-permute-done | bytes 1179680 | tf_op jit(solution)/shard_map/ppermute | solution.py:13
  227.4 4.2 collective-permute-done.3
  231.5 7.6 %pad_maximum_fusion = bf16[8,2,24,24,384]{4,3,2,1,0:T(8,128)(2,1)} fusion(bf16[8,2,24,4,384]{4,3,2,1,0:T(4,128)(2,1)S(1)} %collective-permute-done.3, bf16[8,2,4,16,384]{4,3,2,1,0:T(8,128)(2,1)} %collective-permute-done.1, bf16[8,2,16,16,384]{4,3,2,1,0:T(8,128)(2,1)S(1)} %bitcast.71, bf16[8,2,4,16,384]{4,3,2,1,0:T(8,128)(2,1)S(1)} %collective-permute-done, ...), kind=kLoop, calls=%fused_computation.45 | loop fusion | flops 35389440 | bytes 14155776 | tf_op jit(solution)/shard_map/concatenate | solution.py:48
  239.1 221.7 %while.18 = (s32[]{:T(128)}, f32[4,3,128]{2,1,0:T(4,128)S(1)}, f32[4,3,128]{2,1,0:T(4,128)S(1)}, f32[4,3,128,128]{3,2,1,0:T(8,128)}, s32[8]{0:T(128)S(1)}, /*ind...) while((s32[]{:T(128)}, f32[4,3,128]{2,1,0:T(4,128)S(1)}, ...), condition=%wide.region_3.4_spmd.clone, body=%wide.region_0.3_spmd.clone.sunk | while | flops 421338624 | bytes 41597296 | solution.py:164
  250.4 4.0 fusion.64
  262.2 4.4 fusion.68
  289.7 4.7 fusion.68
  317.4 4.7 fusion.68
  333.4 4.0 fusion.64
  345.2 4.7 fusion.68
  361.2 4.0 fusion.64
  372.9 4.7 fusion.68
  388.9 4.0 fusion.64
  400.7 4.7 fusion.68
  416.6 4.0 fusion.64
  428.4 4.7 fusion.68
  444.4 4.0 fusion.64
  456.1 4.7 fusion.68
  465.2 45.7 %reduce-scatter.2.cloned.1.call-done = bf16[128,1536]{1,0:T(8,128)(2,1)} async-done(((bf16[512,1536]{1,0:T(8,128)(2,1)}), bf16[128,1536]{1,0:T(8,128)(2,1)}) %reduce-scatter.2.cloned.1.call-update) | async-done | bytes 393232 | tf_op jit(solution)/shard_map/reduce_scatter | solution.py:171
  (322 shorter events, 203.3 us)
Async XLA Ops:
  6.5 456.4 %copy-start = (bf16[384,1536]{1,0:T(8,128)(2,1)S(1)}, bf16[384,1536]{1,0:T(8,128)(2,1)}, u32[]{:S(2)}) copy-start(bf16[384,1536]{1,0:T(8,128)(2,1)} %param.13) | copy-start | bytes 3538948
  6.5 86.7 %all-gather.7.cloned.1.call-start = ((), (), s32[]{:S(2)}) async-start(), calls=%async_computation.3 | async-start | bytes 3538944 | tf_op jit(solution)/shard_map/all_gather | solution.py:123
  7.3 162.2 %all-gather.5.cloned.1.call-start = ((), (), s32[]{:S(2)}) async-start(), calls=%async_computation.2 | async-start | bytes 3538944 | tf_op jit(solution)/shard_map/all_gather | solution.py:122
  8.0 502.9 %reduce-scatter.2.cloned.1.call-start = ((), (), s32[]{:S(2)}) async-start(), calls=%async_computation.1 | async-start | bytes 1966080 | tf_op jit(solution)/shard_map/reduce_scatter | solution.py:171
  95.7 20.8 %collective-permute-start.4 = (bf16[8,2,4,16,384]{4,3,2,1,0:T(8,128)(2,1)}, bf16[8,2,4,16,384]{4,3,2,1,0:T(8,128)(2,1)S(1)}, u32[]{:S(2)}, u32[]{:S(2)}) collective-permute-start(bf16[8,2,4,16,384]{4,3,2,1,0:T(8,128)(2,1)} %get-tuple-element.310), channel_id=1, source_target_pairs={{0,16},{4,20},{8,24},{12,28},{16,32},{20,36},{24,40},{28,44},{32,4... | collective-permute-start | bytes 2359304 | tf_op jit(solution)/shard_map/ppermute | solution.py:13
  99.5 20.6 %collective-permute-start.5 = (bf16[8,2,4,16,384]{4,3,2,1,0:T(8,128)(2,1)S(1)}, bf16[8,2,4,16,384]{4,3,2,1,0:T(8,128)(2,1)S(1)}, u32[]{:S(2)}, u32[]{:S(2)}) collective-permute-start(bf16[8,2,4,16,384]{4,3,2,1,0:T(8,128)(2,1)S(1)} %get-tuple-element.311), channel_id=1, source_target_pairs={{16,0},{20,4},{24,8},{28,12},{32,16},{36,20},{40,24},{44,28},{48,3... | collective-permute-start | bytes 2359304 | tf_op jit(solution)/shard_map/ppermute | solution.py:13
  123.6 81.5 %collective-permute-start.6 = (bf16[8,2,24,4,384]{4,3,2,1,0:T(4,128)(2,1)}, bf16[8,2,24,4,384]{4,3,2,1,0:T(4,128)(2,1)}, u32[]{:S(2)}, u32[]{:S(2)}) collective-permute-start(bf16[8,2,24,4,384]{4,3,2,1,0:T(4,128)(2,1)} %get-tuple-element.306), channel_id=1, source_target_pairs={{0,4},{4,8},{8,12},{12,16},{16,20},{20,24},{24,28},{28,32},{32,36}... | collective-permute-start | bytes 3538952 | tf_op jit(solution)/shard_map/ppermute | solution.py:13
  127.8 77.3 %collective-permute-start.7 = (bf16[8,2,24,4,384]{4,3,2,1,0:T(4,128)(2,1)}, bf16[8,2,24,4,384]{4,3,2,1,0:T(4,128)(2,1)}, u32[]{:S(2)}, u32[]{:S(2)}) collective-permute-start(bf16[8,2,24,4,384]{4,3,2,1,0:T(4,128)(2,1)} %get-tuple-element.307), channel_id=1, source_target_pairs={{4,0},{8,4},{12,8},{16,12},{20,16},{24,20},{28,24},{32,28},{36,32}... | collective-permute-start | bytes 3538952 | tf_op jit(solution)/shard_map/ppermute | solution.py:13
  172.2 24.9 %collective-permute-start = (bf16[8,2,4,16,384]{4,3,2,1,0:T(8,128)(2,1)}, bf16[8,2,4,16,384]{4,3,2,1,0:T(8,128)(2,1)S(1)}, u32[]{:S(2)}, u32[]{:S(2)}) collective-permute-start(bf16[8,2,4,16,384]{4,3,2,1,0:T(8,128)(2,1)} %get-tuple-element.312), channel_id=1, source_target_pairs={{0,16},{4,20},{8,24},{12,28},{16,32},{20,36},{24,40},{28,44},{32,4... | collective-permute-start | bytes 2359304 | tf_op jit(solution)/shard_map/ppermute | solution.py:13
  176.1 21.1 %collective-permute-start.1 = (bf16[8,2,4,16,384]{4,3,2,1,0:T(8,128)(2,1)}, bf16[8,2,4,16,384]{4,3,2,1,0:T(8,128)(2,1)}, u32[]{:S(2)}, u32[]{:S(2)}) collective-permute-start(bf16[8,2,4,16,384]{4,3,2,1,0:T(8,128)(2,1)} %get-tuple-element.313), channel_id=1, source_target_pairs={{16,0},{20,4},{24,8},{28,12},{32,16},{36,20},{40,24},{44,28},{48,3... | collective-permute-start | bytes 2359304 | tf_op jit(solution)/shard_map/ppermute | solution.py:13
  197.2 7.9 %copy-start.2 = (bf16[8,1,2,16,16,384]{5,4,3,2,1,0:T(8,128)(2,1)S(1)}, bf16[8,1,2,16,16,384]{5,4,3,2,1,0:T(8,128)(2,1)}, u32[]{:S(2)}) copy-start(bf16[8,1,2,16,16,384]{5,4,3,2,1,0:T(8,128)(2,1)} %all-gather.7.cloned.1.call-done) | copy-start | bytes 9437188
  200.1 27.2 %collective-permute-start.2 = (bf16[8,2,24,4,384]{4,3,2,1,0:T(4,128)(2,1)S(1)}, bf16[8,2,24,4,384]{4,3,2,1,0:T(4,128)(2,1)S(1)}, u32[]{:S(2)}, u32[]{:S(2)}) collective-permute-start(bf16[8,2,24,4,384]{4,3,2,1,0:T(4,128)(2,1)S(1)} %get-tuple-element.308), channel_id=1, source_target_pairs={{0,4},{4,8},{8,12},{12,16},{16,20},{20,24},{24,28},{28,32},{32,36}... | collective-permute-start | bytes 3538952 | tf_op jit(solution)/shard_map/ppermute | solution.py:13
  203.3 28.2 %copy-start.1 = (bf16[8,1,2,16,16,384]{5,4,3,2,1,0:T(8,128)(2,1)S(1)}, bf16[8,1,2,16,16,384]{5,4,3,2,1,0:T(8,128)(2,1)}, u32[]{:S(2)}) copy-start(bf16[8,1,2,16,16,384]{5,4,3,2,1,0:T(8,128)(2,1)} %all-gather.5.cloned.1.call-done) | copy-start | bytes 9437188
  203.3 28.2 %collective-permute-start.3 = (bf16[8,2,24,4,384]{4,3,2,1,0:T(4,128)(2,1)S(1)}, bf16[8,2,24,4,384]{4,3,2,1,0:T(4,128)(2,1)S(1)}, u32[]{:S(2)}, u32[]{:S(2)}) collective-permute-start(bf16[8,2,24,4,384]{4,3,2,1,0:T(4,128)(2,1)S(1)} %get-tuple-element.309), channel_id=1, source_target_pairs={{4,0},{8,4},{12,8},{16,12},{20,16},{24,20},{28,24},{32,28},{36,32}... | collective-permute-start | bytes 3538952 | tf_op jit(solution)/shard_map/ppermute | solution.py:13
  250.4 4.0 copy-start.5
  260.1 1.9 copy-start.3
  277.9 4.0 copy-start.5
  287.6 1.9 copy-start.3
  305.7 4.0 copy-start.5
  333.4 4.0 copy-start.5
  361.1 4.0 copy-start.5
  388.9 4.0 copy-start.5
  416.6 4.0 copy-start.5
  444.4 4.0 copy-start.5
  (23 other events, 36.3 us)
Sparse Core Ops, SparseCore 0:
  9.5 83.6 all-gather.6
  95.3 74.1 all-gather.4
  465.3 45.5 reduce-scatter.1
where the time goes:
time: 520 us; the launch traced here: 517 us
  waiting for transfers between devices  209 us (40%)
  local copies, waits for them, and re-layouts  134 us (26%)
  matrix products  71.3 us (14%)
  other arithmetic  53.4 us (10%)
  starting transfers between devices  20.7 us (4%)
  loops' own time  15.8 us (3%)
  between operations  13.3 us (3%)
    all_gather x1, waiting for transfers between devices, per_device(): lax.all_gather(values[0], 'tm', axis=0, tiled=True)  85.1 us
    another operation x128, local copies, waits for them, and re-layouts, windows_of(): stacked = jnp.stack(parts)  77.2 us
    reduce_scatter x1, waiting for transfers between devices, per_device(): lax.psum_scatter(jnp.dot(attn, out_weight, preferred_element_type=jnp.flo...  45.7 us
    all_gather x1, waiting for transfers between devices, per_device(): lax.all_gather(keys[0], 'tm', axis=0, tiled=True)  40.4 us
    dot_general x8, matrix products, one_stretch(): jnp.einsum('nhqk,nkhd->nhqd', probs.astype(jnp.bfloat16), value_win, pref...  37.1 us
    ppermute x8, waiting for transfers between devices, passed_along(): return lax.ppermute(value, axis, pairs)  36.7 us
    dot_general x8, matrix products, one_stretch(): jnp.einsum('nqhd,nkhd->nhqk', queries, key_win, preferred_element_type=jn...  32 us
    ppermute x8, starting transfers between devices, passed_along(): return lax.ppermute(value, axis, pairs)  20.6 us
  transfers between devices with their start and end apart: 11, of which 7 were waited for; matrix products, arithmetic and copies ran while one was open for 8% of the time, Pallas kernels for 0%

commit v1 on v0

--- a/solution.py
+++ b/solution.py
@@ -120,7 +120,9 @@
 
     key_all, value_all = (
         lax.all_gather(keys[0], "tm", axis=0, tiled=True),
-        lax.all_gather(values[0], "tm", axis=0, tiled=True),
+        jnp.concatenate(
+            lax.all_to_all(jnp.stack([values[0]] * lax.axis_size("tm")), "tm", 0, 0), axis=0
+        ),
     )
     key_full, value_full = widen(key_all, value_all, span, all_row_move, all_col_move)
     piece = (key_full, value_full)

time: 520 us -> 621 us (1.19)
  waiting for transfers between devices: 209 us -> 292 us
  starting transfers between devices: 20.7 us -> 35.7 us
    all_gather x1, waiting for transfers between devices: 40.4 us -> 197 us  [per_device(): lax.all_gather(keys[0], 'tm', axis=0, tiled=True)]
    all_gather x1 -> x0, waiting for transfers between devices: 85.1 us -> none  [per_device(): lax.all_gather(values[0], 'tm', axis=0, tiled=True)]
    all_to_all x0 -> x1, starting transfers between devices: none -> 16.6 us  [per_device(): lax.all_to_all(jnp.stack([values[0]] * lax.axis_size('tm')), 'tm', 0, 0)]
    ppermute x8, waiting for transfers between devices: 36.7 us -> 50.7 us  [passed_along(): return lax.ppermute(value, axis, pairs)]
  transfers between devices with their start and end apart: 11 -> 11, of which waited for: 7 -> 7; matrix products, arithmetic and copies ran while one was open for 8% -> 6% of each run, Pallas kernels for 0% -> 0%
where the time goes in v1:
time: 621 us; the launch traced here: 618 us
  waiting for transfers between devices  292 us (47%)
  local copies, waits for them, and re-layouts  137 us (22%)
  matrix products  71.3 us (11%)
  other arithmetic  54.2 us (9%)
  starting transfers between devices  35.7 us (6%)
  loops' own time  14.3 us (2%)
  between operations  13.6 us (2%)
    all_gather x1, waiting for transfers between devices, per_device(): lax.all_gather(keys[0], 'tm', axis=0, tiled=True)  197 us
    another operation x128, local copies, waits for them, and re-layouts, windows_of(): stacked = jnp.stack(parts)  77.3 us
    ppermute x8, waiting for transfers between devices, passed_along(): return lax.ppermute(value, axis, pairs)  50.7 us
    reduce_scatter x1, waiting for transfers between devices, per_device(): lax.psum_scatter(jnp.dot(attn, out_weight, preferred_element_type=jnp.flo...  44 us
    dot_general x8, matrix products, one_stretch(): jnp.einsum('nhqk,nkhd->nhqd', probs.astype(jnp.bfloat16), value_win, pref...  37.1 us
    dot_general x8, matrix products, one_stretch(): jnp.einsum('nqhd,nkhd->nhqk', queries, key_win, preferred_element_type=jn...  32 us
    reduce_sum x8, other arithmetic, one_stretch(): total = total * shrink + jnp.sum(probs, axis=3)  19.6 us
    ppermute x8, starting transfers between devices, passed_along(): return lax.ppermute(value, axis, pairs)  19.1 us
  transfers between devices with their start and end apart: 11, of which 7 were waited for; matrix products, arithmetic and copies ran while one was open for 6% of the time, Pallas kernels for 0%

profile of v1, /device:TPU:1, one launch (start us, length us, event | category | flops | bytes accessed | tf_op | source)
XLA Modules:
  0.0 618.0 jit_solution(15428805428925460804)
XLA Ops:
  9.7 16.6 %all-to-all-start = ((bf16[8,1,2,16,16,384]{5,4,3,2,1,0:T(8,128)(2,1)}), bf16[8,1,2,16,16,384]{5,4,3,2,1,0:T(8,128)(2,1)}, u32[]{:S(2)}, u32[]{:S(2)}) async-start(bf16[8,1,2,16,16,384]{5,4,3,2,1,0:T(8,128)(2,1)} %stack.33), calls=%async_computation | async-start | bytes 6291456 | tf_op jit(solution)/shard_map/all_to_all | solution.py:124
  27.1 196.8 %all-gather.3.cloned.1.call-done = bf16[8,1,2,16,16,384]{5,4,3,2,1,0:T(8,128)(2,1)} async-done(((bf16[1,1,2,16,16,384]{5,4,3,2,1,0:T(8,128)(2,1)}), bf16[8,1,2,16,16,384]{5,4,3,2,1,0:T(8,128)(2,1)}) %all-gather.3.cloned.1.call-update) | async-done | bytes 3145744 | tf_op jit(solution)/shard_map/all_gather | solution.py:122
  232.1 14.3 %collective-permute-done = bf16[8,2,4,16,384]{4,3,2,1,0:T(8,128)(2,1)S(1)} collective-permute-done((bf16[8,2,4,16,384]{4,3,2,1,0:T(8,128)(2,1)}, bf16[8,2,4,16,384]{4,3,2,1,0:T(8,128)(2,1)S(1)}, u32[]{:S(2)}, u32[]{:S(2)}) %collective-permute-start) | collective-permute-done | bytes 786464 | tf_op jit(solution)/shard_map/ppermute | solution.py:13
  253.5 4.3 collective-permute-start.2
  261.9 4.9 collective-permute-start.4
  288.1 15.4 %collective-permute-done.5 = bf16[8,2,4,16,384]{4,3,2,1,0:T(8,128)(2,1)} collective-permute-done((bf16[8,2,4,16,384]{4,3,2,1,0:T(8,128)(2,1)}, bf16[8,2,4,16,384]{4,3,2,1,0:T(8,128)(2,1)}, u32[]{:S(2)}, u32[]{:S(2)}) %collective-permute-start.5) | collective-permute-done | bytes 786464 | tf_op jit(solution)/shard_map/ppermute | solution.py:13
  309.2 7.7 %pad_maximum_fusion = bf16[8,2,24,24,384]{4,3,2,1,0:T(8,128)(2,1)} fusion(bf16[8,2,24,4,384]{4,3,2,1,0:T(4,128)(2,1)} %collective-permute-done.3, bf16[8,2,4,16,384]{4,3,2,1,0:T(8,128)(2,1)S(1)} %collective-permute-done.1, bf16[8,2,16,16,384]{4,3,2,1,0:T(8,128)(2,1)S(1)} %bitcast.72, bf16[8,2,4,16,384]{4,3,2,1,0:T(8,128)(2,1)S(1)} %collective-permute-done, ...), kind=kLoop, calls=%fused_computation.45 | loop fusion | flops 35389440 | bytes 14155776 | tf_op jit(solution)/shard_map/concatenate | solution.py:48
  316.9 13.6 %collective-permute-done.6 = bf16[8,2,24,4,384]{4,3,2,1,0:T(4,128)(2,1)S(1)} collective-permute-done((bf16[8,2,24,4,384]{4,3,2,1,0:T(4,128)(2,1)S(1)}, bf16[8,2,24,4,384]{4,3,2,1,0:T(4,128)(2,1)S(1)}, u32[]{:S(2)}, u32[]{:S(2)}) %collective-permute-start.6) | collective-permute-done | bytes 1179680 | tf_op jit(solution)/shard_map/ppermute | solution.py:13
  334.4 8.4 %pad_maximum_fusion.1 = bf16[8,2,24,24,384]{4,3,2,1,0:T(8,128)(2,1)} fusion(bf16[8,2,24,4,384]{4,3,2,1,0:T(4,128)(2,1)S(1)} %collective-permute-done.7, bf16[8,2,4,16,384]{4,3,2,1,0:T(8,128)(2,1)} %collective-permute-done.5, bf16[8,2,16,16,384]{4,3,2,1,0:T(8,128)(2,1)} %bitcast.4, bf16[8,2,4,16,384]{4,3,2,1,0:T(8,128)(2,1)S(1)} %collective-permute-done.4, ...), kind=kLoop, calls=%fused_computation.46 | loop fusion | flops 35389440 | bytes 14155776 | tf_op jit(solution)/shard_map/concatenate | solution.py:49
  342.8 220.0 %while.18 = (s32[]{:T(128)}, f32[4,3,128]{2,1,0:T(4,128)S(1)}, f32[4,3,128]{2,1,0:T(4,128)S(1)}, f32[4,3,128,128]{3,2,1,0:T(8,128)}, s32[8]{0:T(128)S(1)}, /*ind...) while((s32[]{:T(128)}, f32[4,3,128]{2,1,0:T(4,128)S(1)}, ...), condition=%wide.region_3.4_spmd.clone, body=%wide.region_0.3_spmd.clone.sunk | while | flops 421338624 | bytes 41597296 | solution.py:166
  353.9 4.0 fusion.64
  365.7 4.4 fusion.68
  393.0 4.7 fusion.68
  408.7 4.0 fusion.64
  420.5 4.7 fusion.68
  448.0 4.7 fusion.68
  463.8 4.0 fusion.64
  475.6 4.7 fusion.68
  491.3 4.0 fusion.64
  503.1 4.7 fusion.68
  518.9 4.0 fusion.64
  530.6 4.7 fusion.68
  558.2 4.7 fusion.68
  567.2 44.0 %reduce-scatter.2.cloned.1.call-done = bf16[128,1536]{1,0:T(8,128)(2,1)} async-done(((bf16[512,1536]{1,0:T(8,128)(2,1)}), bf16[128,1536]{1,0:T(8,128)(2,1)}) %reduce-scatter.2.cloned.1.call-update) | async-done | bytes 393232 | tf_op jit(solution)/shard_map/reduce_scatter | solution.py:173
  (320 shorter events, 206.9 us)
Async XLA Ops:
  6.5 558.5 %copy-start = (bf16[384,1536]{1,0:T(8,128)(2,1)S(1)}, bf16[384,1536]{1,0:T(8,128)(2,1)}, u32[]{:S(2)}) copy-start(bf16[384,1536]{1,0:T(8,128)(2,1)} %param.13) | copy-start | bytes 3538948
  9.7 249.4 %all-to-all-start = ((bf16[8,1,2,16,16,384]{5,4,3,2,1,0:T(8,128)(2,1)}), bf16[8,1,2,16,16,384]{5,4,3,2,1,0:T(8,128)(2,1)}, u32[]{:S(2)}, u32[]{:S(2)}) async-start(bf16[8,1,2,16,16,384]{5,4,3,2,1,0:T(8,128)(2,1)} %stack.33), calls=%async_computation | async-start | bytes 6291456 | tf_op jit(solution)/shard_map/all_to_all | solution.py:124
  26.3 197.6 %all-gather.3.cloned.1.call-start = ((), (), s32[]{:S(2)}) async-start(), calls=%async_computation.3 | async-start | bytes 3538944 | tf_op jit(solution)/shard_map/all_gather | solution.py:122
  27.0 584.2 %reduce-scatter.2.cloned.1.call-start = ((), (), s32[]{:S(2)}) async-start(), calls=%async_computation.2 | async-start | bytes 1966080 | tf_op jit(solution)/shard_map/reduce_scatter | solution.py:173
  226.4 20.1 %collective-permute-start = (bf16[8,2,4,16,384]{4,3,2,1,0:T(8,128)(2,1)}, bf16[8,2,4,16,384]{4,3,2,1,0:T(8,128)(2,1)S(1)}, u32[]{:S(2)}, u32[]{:S(2)}) collective-permute-start(bf16[8,2,4,16,384]{4,3,2,1,0:T(8,128)(2,1)} %get-tuple-element.312), channel_id=1, source_target_pairs={{0,16},{4,20},{8,24},{12,28},{16,32},{20,36},{24,40},{28,44},{32,4... | collective-permute-start | bytes 2359304 | tf_op jit(solution)/shard_map/ppermute | solution.py:13
  229.5 20.4 %collective-permute-start.1 = (bf16[8,2,4,16,384]{4,3,2,1,0:T(8,128)(2,1)S(1)}, bf16[8,2,4,16,384]{4,3,2,1,0:T(8,128)(2,1)S(1)}, u32[]{:S(2)}, u32[]{:S(2)}) collective-permute-start(bf16[8,2,4,16,384]{4,3,2,1,0:T(8,128)(2,1)S(1)} %get-tuple-element.313), channel_id=1, source_target_pairs={{16,0},{20,4},{24,8},{28,12},{32,16},{36,20},{40,24},{44,28},{48,3... | collective-permute-start | bytes 2359304 | tf_op jit(solution)/shard_map/ppermute | solution.py:13
  253.5 55.7 %collective-permute-start.2 = (bf16[8,2,24,4,384]{4,3,2,1,0:T(4,128)(2,1)}, bf16[8,2,24,4,384]{4,3,2,1,0:T(4,128)(2,1)}, u32[]{:S(2)}, u32[]{:S(2)}) collective-permute-start(bf16[8,2,24,4,384]{4,3,2,1,0:T(4,128)(2,1)} %get-tuple-element.308), channel_id=1, source_target_pairs={{0,4},{4,8},{8,12},{12,16},{16,20},{20,24},{24,28},{28,32},{32,36}... | collective-permute-start | bytes 3538952 | tf_op jit(solution)/shard_map/ppermute | solution.py:13
  257.8 51.3 %collective-permute-start.3 = (bf16[8,2,24,4,384]{4,3,2,1,0:T(4,128)(2,1)}, bf16[8,2,24,4,384]{4,3,2,1,0:T(4,128)(2,1)}, u32[]{:S(2)}, u32[]{:S(2)}) collective-permute-start(bf16[8,2,24,4,384]{4,3,2,1,0:T(4,128)(2,1)} %get-tuple-element.309), channel_id=1, source_target_pairs={{4,0},{8,4},{12,8},{16,12},{20,16},{24,20},{28,24},{32,28},{36,32}... | collective-permute-start | bytes 3538952 | tf_op jit(solution)/shard_map/ppermute | solution.py:13
  261.9 26.2 %collective-permute-start.4 = (bf16[8,2,4,16,384]{4,3,2,1,0:T(8,128)(2,1)}, bf16[8,2,4,16,384]{4,3,2,1,0:T(8,128)(2,1)S(1)}, u32[]{:S(2)}, u32[]{:S(2)}) collective-permute-start(bf16[8,2,4,16,384]{4,3,2,1,0:T(8,128)(2,1)} %get-tuple-element.310), channel_id=1, source_target_pairs={{0,16},{4,20},{8,24},{12,28},{16,32},{20,36},{24,40},{28,44},{32,4... | collective-permute-start | bytes 2359304 | tf_op jit(solution)/shard_map/ppermute | solution.py:13
  266.8 36.7 %collective-permute-start.5 = (bf16[8,2,4,16,384]{4,3,2,1,0:T(8,128)(2,1)}, bf16[8,2,4,16,384]{4,3,2,1,0:T(8,128)(2,1)}, u32[]{:S(2)}, u32[]{:S(2)}) collective-permute-start(bf16[8,2,4,16,384]{4,3,2,1,0:T(8,128)(2,1)} %get-tuple-element.311), channel_id=1, source_target_pairs={{16,0},{20,4},{24,8},{28,12},{32,16},{36,20},{40,24},{44,28},{48,3... | collective-permute-start | bytes 2359304 | tf_op jit(solution)/shard_map/ppermute | solution.py:13
  288.1 21.0 %copy-start.1 = (bf16[8,1,2,16,16,384]{5,4,3,2,1,0:T(8,128)(2,1)S(1)}, bf16[8,1,2,16,16,384]{5,4,3,2,1,0:T(8,128)(2,1)}, u32[]{:S(2)}) copy-start(bf16[8,1,2,16,16,384]{5,4,3,2,1,0:T(8,128)(2,1)} %all-gather.3.cloned.1.call-done) | copy-start | bytes 9437188
  306.3 24.2 %collective-permute-start.6 = (bf16[8,2,24,4,384]{4,3,2,1,0:T(4,128)(2,1)S(1)}, bf16[8,2,24,4,384]{4,3,2,1,0:T(4,128)(2,1)S(1)}, u32[]{:S(2)}, u32[]{:S(2)}) collective-permute-start(bf16[8,2,24,4,384]{4,3,2,1,0:T(4,128)(2,1)S(1)} %get-tuple-element.306), channel_id=1, source_target_pairs={{0,4},{4,8},{8,12},{12,16},{16,20},{20,24},{24,28},{28,32},{32,36}... | collective-permute-start | bytes 3538952 | tf_op jit(solution)/shard_map/ppermute | solution.py:13
  307.7 26.7 %collective-permute-start.7 = (bf16[8,2,24,4,384]{4,3,2,1,0:T(4,128)(2,1)S(1)}, bf16[8,2,24,4,384]{4,3,2,1,0:T(4,128)(2,1)S(1)}, u32[]{:S(2)}, u32[]{:S(2)}) collective-permute-start(bf16[8,2,24,4,384]{4,3,2,1,0:T(4,128)(2,1)S(1)} %get-tuple-element.307), channel_id=1, source_target_pairs={{4,0},{8,4},{12,8},{16,12},{20,16},{24,20},{28,24},{32,28},{36,32}... | collective-permute-start | bytes 3538952 | tf_op jit(solution)/shard_map/ppermute | solution.py:13
  353.9 4.0 copy-start.4
  381.2 4.0 copy-start.4
  390.9 1.9 copy-start.2
  408.7 4.0 copy-start.4
  418.5 1.9 copy-start.2
  436.3 4.0 copy-start.4
  463.8 4.0 copy-start.4
  473.5 1.9 copy-start.2
  491.3 4.0 copy-start.4
  518.9 4.0 copy-start.4
  546.4 4.0 copy-start.4
  (22 other events, 34.5 us)
Sparse Core Ops, SparseCore 0:
  29.2 194.5 all-gather.2
  567.3 43.8 reduce-scatter.1
